TPU v7x, 32 devices: a whole 2x2x4 slice. The times are simulated.
32 devices in a mesh: ctx: 32 (over z, y, x, core), head: 1.
Axes of the slice: x: 2, y: 2, z: 4, core: 2. Of those that a mesh axis runs over, the one named last changes fastest.
Arguments:
- queries: bfloat16 [6144, 4096], P('ctx', 'head'), may hold values from -96 to 96
- key_rows: bfloat16 [6144, 4096], P('ctx', 'head'), may hold values from -8 to 8
- value_rows: bfloat16 [6144, 4096], P('ctx', 'head'), may hold values from -6 to 6
- token_rates: float32 [6144, 8], P('ctx', 'head'), may hold values from 0.02 to 1
- fast_one: bfloat16 [8, 512, 512], P('head'), may hold values from -0.25 to 0.25
- fast_three: bfloat16 [8, 512, 512], P('head'), may hold values from -0.25 to 0.25
- fast_two: bfloat16 [8, 512, 512], P('head'), may hold values from -0.25 to 0.25
- head_gain: float32 [8], P('head'), may hold values from 0.5 to 1.5
Outputs:
- window_out: bfloat16 [6144, 4096], P('ctx', 'head')
- fast_out: bfloat16 [6144, 4096], P('ctx', 'head')
All inputs are finite; a program needn't handle non-finite values.
Results may differ from a plain program's by a relative error of at most 0.011.
Values may be sent and summed in bfloat16 or wider, within the bound.
A program may use at most 128 MiB of HBM per device.

v0:
```python
import jax
import jax.numpy as jnp
from jax import lax
from jax.sharding import PartitionSpec as P

HEADS = 8
HD = 512
WINDOW = 1024
NS_STEPS = 2


COEF_A = 3.4445
COEF_B = -4.775
COEF_C = 2.0315
EPSILON = 1e-06


def passed_along(x, axis, by):
    peers = lax.axis_size(axis)
    pairs = [(i, i + by) for i in range(peers) if 0 <= i + by < peers]
    return lax.ppermute(x, axis, pairs)


def rms_heads(block):
    return block / jnp.sqrt(jnp.mean(block * block, axis=-1, keepdims=True) + EPSILON)


def window_attention(split_q, split_k, split_v):
    tokens_here = split_q.shape[0]
    span = (WINDOW + tokens_here - 2) // tokens_here
    paired = jnp.stack([split_k, split_v])
    earlier = []
    current = paired
    for distance in range(span):
        current = passed_along(current, "ctx", 1)
        earlier.insert(0, current)
    window_pairs = jnp.concatenate(earlier + [paired], axis=1)
    key_count = window_pairs.shape[1]
    scores = jnp.einsum(
        "qhd,khd->hqk", split_q, window_pairs[0], preferred_element_type=jnp.float32
    ) * split_q.shape[2] ** (-0.5)
    query_pos = lax.broadcasted_iota(jnp.int32, (tokens_here, key_count), 0) + span * tokens_here
    key_pos = lax.broadcasted_iota(jnp.int32, (tokens_here, key_count), 1)
    offset = query_pos - key_pos
    first_key = lax.axis_index("ctx") * tokens_here - span * tokens_here
    allowed = (offset >= 0) & (offset < WINDOW) & (key_pos + first_key >= 0)
    scores = jnp.where(allowed[None], scores, -1e30)
    row_top = jnp.max(scores, axis=-1, keepdims=True)
    exponent = jnp.exp(scores - row_top)
    weights = (exponent / jnp.sum(exponent, axis=-1, keepdims=True)).astype(jnp.bfloat16)
    return jnp.einsum("hqk,khd->qhd", weights, window_pairs[1], preferred_element_type=jnp.float32)


def start_iterate(gradient, squares):
    return lax.optimization_barrier(
        (gradient / (jnp.sqrt(squares)[:, None, None] + 1e-07)).astype(jnp.bfloat16)
    )


def mix_rows(piece_rows, gram_rows, gram_whole, whole_matrix):
    mixer = (
        COEF_B * gram_rows.astype(jnp.float32)
        + COEF_C
        * jnp.einsum("hrs,hst->hrt", gram_rows, gram_whole, preferred_element_type=jnp.float32)
    ).astype(jnp.bfloat16)
    return lax.optimization_barrier(
        (
            COEF_A * piece_rows.astype(jnp.float32)
            + jnp.einsum("hrs,hsc->hrc", mixer, whole_matrix, preferred_element_type=jnp.float32)
        ).astype(jnp.bfloat16)
    )


def gram_of(piece_rows, whole_matrix):
    return lax.optimization_barrier(
        jnp.einsum(
            "hrc,hsc->hrs", piece_rows, whole_matrix, preferred_element_type=jnp.float32
        ).astype(jnp.bfloat16)
    )


def orthogonalize(gradient_one, gradient_three, gradient_two):
    summed = lax.psum((gradient_one, gradient_three, gradient_two), "ctx")
    current = [start_iterate(matrix, jnp.sum(matrix * matrix, axis=(1, 2))) for matrix in summed]
    for sweep_index in range(NS_STEPS):
        updated = []
        for matrix in current:
            gram_full = gram_of(matrix, matrix)
            updated.append(mix_rows(matrix, gram_full, gram_full, matrix))
        current = updated
    return current


def fast_weights(split_q, split_k, split_v, token_rates, fast_one, fast_three, fast_two):
    key_normed = rms_heads(split_k.astype(jnp.float32)).astype(jnp.bfloat16)
    query_normed = rms_heads(split_q.astype(jnp.float32)).astype(jnp.bfloat16)
    hidden_one = jnp.einsum(
        "thd,hdf->thf", key_normed, fast_one, preferred_element_type=jnp.float32
    )
    hidden_three = jnp.einsum(
        "thd,hdf->thf", key_normed, fast_three, preferred_element_type=jnp.float32
    )
    sigmoid_one = jax.nn.sigmoid(hidden_one)
    active = hidden_one * sigmoid_one
    hidden = (active * hidden_three).astype(jnp.bfloat16)
    delta_out = (-token_rates[:, :, None] * split_v.astype(jnp.float32)).astype(jnp.bfloat16)
    delta_hidden = jnp.einsum(
        "thd,hfd->thf", delta_out, fast_two, preferred_element_type=jnp.float32
    )
    delta_three = (delta_hidden * active).astype(jnp.bfloat16)
    delta_one = (
        delta_hidden * hidden_three * sigmoid_one * (1.0 + hidden_one * (1.0 - sigmoid_one))
    ).astype(jnp.bfloat16)
    gradient_one = jnp.einsum(
        "thd,thf->hdf", key_normed, delta_one, preferred_element_type=jnp.float32
    )
    gradient_three = jnp.einsum(
        "thd,thf->hdf", key_normed, delta_three, preferred_element_type=jnp.float32
    )
    gradient_two = jnp.einsum("thf,thd->hfd", hidden, delta_out, preferred_element_type=jnp.float32)
    solved = orthogonalize(gradient_one, gradient_three, gradient_two)
    new_one = (fast_one.astype(jnp.float32) - solved[0].astype(jnp.float32)).astype(jnp.bfloat16)
    new_three = (fast_three.astype(jnp.float32) - solved[1].astype(jnp.float32)).astype(
        jnp.bfloat16
    )
    new_two = (fast_two.astype(jnp.float32) - solved[2].astype(jnp.float32)).astype(jnp.bfloat16)
    query_one = jnp.einsum(
        "thd,hdf->thf", query_normed, new_one, preferred_element_type=jnp.float32
    )
    query_three = jnp.einsum(
        "thd,hdf->thf", query_normed, new_three, preferred_element_type=jnp.float32
    )
    query_hidden = (jax.nn.silu(query_one) * query_three).astype(jnp.bfloat16)
    return jnp.einsum("thf,hfd->thd", query_hidden, new_two, preferred_element_type=jnp.float32)


def local(queries, key_rows, value_rows, token_rates, fast_one, fast_three, fast_two, head_gain):
    tokens_here = queries.shape[0]
    heads_here = fast_one.shape[0]
    width = fast_one.shape[1]
    split_q = queries.reshape(tokens_here, heads_here, width)
    split_k = key_rows.reshape(tokens_here, heads_here, width)
    split_v = value_rows.reshape(tokens_here, heads_here, width)
    attended = window_attention(split_q, split_k, split_v)
    fast = fast_weights(split_q, split_k, split_v, token_rates, fast_one, fast_three, fast_two)
    fast = fast * head_gain[None, :, None]
    totals = lax.psum(
        (jnp.sum(attended * attended, axis=(1, 2)), jnp.sum(fast * fast, axis=(1, 2))), "head"
    )
    full_width = HEADS * HD
    window_out = attended / jnp.sqrt(totals[0] / full_width + EPSILON)[:, None, None]
    fast_out = fast / jnp.sqrt(totals[1] / full_width + EPSILON)[:, None, None]
    return (
        window_out.reshape(tokens_here, heads_here * width).astype(jnp.bfloat16),
        fast_out.reshape(tokens_here, heads_here * width).astype(jnp.bfloat16),
    )


def solution(mesh):
    return jax.shard_map(
        local,
        mesh=mesh,
        in_specs=(
            P("ctx", "head"),
            P("ctx", "head"),
            P("ctx", "head"),
            P("ctx", "head"),
            P("head", None, None),
            P("head", None, None),
            P("head", None, None),
            P("head"),
        ),
        out_specs=(P("ctx", "head"), P("ctx", "head")),
        check_vma=False,
    )
```

profile of v0, /device:TPU:1, one launch (start us, length us, event | category | flops | bytes accessed | tf_op | source)
XLA Modules:
  0.0 780.9 jit_solution(929031229312565245)
XLA Ops:
  23.7 5.6 fusion.61
  29.3 5.2 fusion.59
  43.7 61.3 %collective-permute-done = bf16[2,192,8,512]{3,1,2,0:T(8,128)(2,1)S(1)} collective-permute-done((bf16[2,192,8,512]{3,1,2,0:T(8,128)(2,1)S(1)}, bf16[2,192,8,512]{3,1,2,0:T(8,128)(2,1)S(1)}, u32[]{:S(2)}, u32[]{:S(2)}) %collective-permute-start) | collective-permute-done | bytes 3145760 | tf_op jit(solution)/shard_map/ppermute | solution.py:21
  111.0 46.9 %collective-permute-done.1 = bf16[2,192,8,512]{3,1,2,0:T(8,128)(2,1)} collective-permute-done((bf16[2,192,8,512]{3,1,2,0:T(8,128)(2,1)S(1)}, bf16[2,192,8,512]{3,1,2,0:T(8,128)(2,1)}, u32[]{:S(2)}, u32[]{:S(2)}) %collective-permute-start.1) | collective-permute-done | bytes 3145760 | tf_op jit(solution)/shard_map/ppermute | solution.py:21
  164.6 36.9 %collective-permute-done.2 = bf16[2,192,8,512]{3,1,2,0:T(8,128)(2,1)} collective-permute-done((bf16[2,192,8,512]{3,1,2,0:T(8,128)(2,1)}, bf16[2,192,8,512]{3,1,2,0:T(8,128)(2,1)}, u32[]{:S(2)}, u32[]{:S(2)}) %collective-permute-start.2) | collective-permute-done | bytes 3145760 | tf_op jit(solution)/shard_map/ppermute | solution.py:21
  201.5 4.8 collective-permute-start.3
  206.3 321.6 %all-reduce.3.cloned.1.call-done = (f32[8,512,512]{2,1,0:T(8,128)}, f32[8,512,512]{2,1,0:T(8,128)}, f32[8,512,512]{2,1,0:T(8,128)}) async-done(((f32[8,512,512]{2,1,0:T(8,128)}, f32[8,512,512]{2,1,0:T(8,128)}, f32[8,512,512]{2,1,0:T(8,128)}), (f32[8,512,512]{2,1,0:T(8,128)}, f32[8,512,512]{2,1,0:T(8,128)}, f32[8,512,512]{2,1,0:T(8,128)})) %all-reduce.3.cloned.1.call-update) | async-done | bytes 25165840 | tf_op jit(solution)/shard_map/psum | solution.py:83
  541.3 13.9 %add_convert_fusion.10 = bf16[8,512,512]{2,1,0:T(8,128)(2,1)} fusion(bf16[8,512,512]{2,1,0:T(8,128)(2,1)} %copy-done.8, bf16[8,512,512]{2,1,0:T(8,128)(2,1)} %convolution_convert_fusion.5), kind=kOutput, calls=%fused_computation.25 | convolution fusion | flops 4313841664 | bytes 12582912 | tf_op jit(solution)/shard_map/hrs,hsc->hrc/dot_general | solution.py:69
  555.2 7.8 %convolution_convert_fusion.4 = bf16[8,512,512]{2,1,0:T(8,128)(2,1)} fusion(bf16[8,512,512]{2,1,0:T(8,128)(2,1)} %add_convert_fusion.10), kind=kOutput, calls=%fused_computation.94 | convolution fusion | flops 2149580800 | bytes 8388608 | tf_op jit(solution)/shard_map/hrc,hsc->hrs/dot_general | solution.py:76
  563.0 14.3 %add_convert_fusion.8 = bf16[8,512,512]{2,1,0:T(8,128)(2,1)} fusion(bf16[8,512,512]{2,1,0:T(8,128)(2,1)} %add_convert_fusion.10, bf16[8,512,512]{2,1,0:T(8,128)(2,1)} %convolution_convert_fusion.4), kind=kOutput, calls=%fused_computation.23 | convolution fusion | flops 4313841664 | bytes 12582912 | tf_op jit(solution)/shard_map/hrs,hsc->hrc/dot_general | solution.py:69
  586.3 6.1 divide_convert_fusion.1
  598.7 13.8 %add_convert_fusion.6 = bf16[8,512,512]{2,1,0:T(8,128)(2,1)} fusion(bf16[8,512,512]{2,1,0:T(8,128)(2,1)} %copy-done.6, bf16[8,512,512]{2,1,0:T(8,128)(2,1)} %convolution_convert_fusion.3), kind=kOutput, calls=%fused_computation.18 | convolution fusion | flops 4313841664 | bytes 12582912 | tf_op jit(solution)/shard_map/hrs,hsc->hrc/dot_general | solution.py:69
  612.5 7.8 %convolution_convert_fusion.2 = bf16[8,512,512]{2,1,0:T(8,128)(2,1)} fusion(bf16[8,512,512]{2,1,0:T(8,128)(2,1)} %add_convert_fusion.6), kind=kOutput, calls=%fused_computation.92 | convolution fusion | flops 2149580800 | bytes 8388608 | tf_op jit(solution)/shard_map/hrc,hsc->hrs/dot_general | solution.py:76
  620.3 13.8 %add_convert_fusion.4 = bf16[8,512,512]{2,1,0:T(8,128)(2,1)} fusion(bf16[8,512,512]{2,1,0:T(8,128)(2,1)} %add_convert_fusion.6, bf16[8,512,512]{2,1,0:T(8,128)(2,1)} %convolution_convert_fusion.2), kind=kOutput, calls=%fused_computation.16 | convolution fusion | flops 4313841664 | bytes 12582912 | tf_op jit(solution)/shard_map/hrs,hsc->hrc/dot_general | solution.py:69
  634.1 8.2 %convolution_convert_fusion.1 = bf16[8,512,512]{2,1,0:T(8,128)(2,1)} fusion(bf16[8,512,512]{2,1,0:T(8,128)(2,1)} %get-tuple-element.9), kind=kOutput, calls=%fused_computation.91 | convolution fusion | flops 2149580800 | bytes 8388608 | tf_op jit(solution)/shard_map/hrc,hsc->hrs/dot_general | solution.py:76
  647.0 13.8 %add_convert_fusion.2 = bf16[8,512,512]{2,1,0:T(8,128)(2,1)} fusion(bf16[8,512,512]{2,1,0:T(8,128)(2,1)} %get-tuple-element.9, bf16[8,512,512]{2,1,0:T(8,128)(2,1)} %convolution_convert_fusion.1), kind=kOutput, calls=%fused_computation.11 | convolution fusion | flops 4313841664 | bytes 12582912 | tf_op jit(solution)/shard_map/hrs,hsc->hrc/dot_general | solution.py:69
  660.8 7.8 %convolution_convert_fusion = bf16[8,512,512]{2,1,0:T(8,128)(2,1)} fusion(bf16[8,512,512]{2,1,0:T(8,128)(2,1)} %add_convert_fusion.2), kind=kOutput, calls=%fused_computation.90 | convolution fusion | flops 2149580800 | bytes 8388608 | tf_op jit(solution)/shard_map/hrc,hsc->hrs/dot_general | solution.py:76
  668.6 14.1 %add_convert_fusion = bf16[8,512,512]{2,1,0:T(8,128)(2,1)} fusion(bf16[8,512,512]{2,1,0:T(8,128)(2,1)} %add_convert_fusion.2, bf16[8,512,512]{2,1,0:T(8,128)(2,1)} %convolution_convert_fusion), kind=kOutput, calls=%fused_computation.9 | convolution fusion | flops 4313841664 | bytes 12582912 | tf_op jit(solution)/shard_map/hrs,hsc->hrc/dot_general | solution.py:69
  686.1 7.0 fusion.13
  693.1 12.3 %multiply_reduce_fusion.3 = (f32[192]{0:T(256)S(1)}, f32[8,512,192]{1,2,0:T(8,128)}) fusion(f32[8]{0:T(128)S(1)} %copy-done.12, bf16[8,512,512]{2,1,0:T(8,128)(2,1)} %add_convert_fusion.8, bf16[8,512,512]{2,1,0:T(8,128)(2,1)} %param.14, f32[8,512,192]{1,2,0:T(8,128)} %fusion.13, bf16[8,512,512]{2,1,0:T(8,128)(2,1)} %add_convert_fusion, ...), kind=kOutput, calls=%fused_computation.85 | convolution fusion | flops 1636826880 | bytes 24648480 | tf_op jit(solution)/shard_map/thf,hfd->thd/dot_general | solution.py:134
  709.2 11.2 %collective-permute-done.5 = bf16[2,192,8,512]{3,1,2,0:T(8,128)(2,1)} collective-permute-done((bf16[2,192,8,512]{3,1,2,0:T(8,128)(2,1)}, bf16[2,192,8,512]{3,1,2,0:T(8,128)(2,1)}, u32[]{:S(2)}, u32[]{:S(2)}) %collective-permute-start.5) | collective-permute-done | bytes 3145760 | tf_op jit(solution)/shard_map/ppermute | solution.py:21
  744.9 11.8 %fusion.2 = f32[8,1344,192]{1,2,0:T(8,128)} fusion(bf16[2,1344,8,512]{3,1,2,0:T(8,128)(2,1)} %constant_dynamic-update-slice_fusion, bf16[24,8,8,512]{3,2,1,0:T(8,128)(2,1)} %bitcast.175), kind=kOutput, calls=%fused_computation.4 | convolution fusion | flops 2113929216 | bytes 20840448 | tf_op jit(solution)/shard_map/qhd,khd->hqk/dot_general | solution.py:39
  756.7 6.4 fusion.107
  763.0 8.9 %multiply_reduce_fusion.5 = (f32[192]{0:T(256)S(1)}, f32[8,512,192]{1,2,0:T(8,128)S(1)}) fusion(bf16[2,1344,8,512]{3,1,2,0:T(8,128)(2,1)} %constant_dynamic-update-slice_fusion, f32[8,192]{1,0:T(8,128)S(1)} %fusion.107, f32[8,1344,192]{1,2,0:T(8,128)} %fusion.2, pred[192,1344]{1,0:T(8,128)(4,1)S(1)} %fusion.71), kind=kOutput, calls=%fused_computation.89 | convolution fusion | flops 2125826560 | bytes 23071488 | tf_op jit(solution)/shard_map/hqk,khd->qhd/dot_general | solution.py:51
  (85 shorter events, 105.1 us)
Async XLA Ops:
  7.2 520.7 %all-reduce.3.cloned.1.call-start = ((), (), s32[]{:S(2)}) async-start(), calls=%async_computation | async-start | bytes 50331648 | tf_op jit(solution)/shard_map/psum | solution.py:83
  9.8 2.2 copy-start.2
  12.0 2.2 copy-start.1
  14.2 1.4 copy-start.4
  15.6 0.7 copy-start.11
  15.6 2.2 copy-start.7
  34.5 1.4 copy-start.3
  35.9 1.4 copy-start.5
  39.2 65.8 %collective-permute-start = (bf16[2,192,8,512]{3,1,2,0:T(8,128)(2,1)S(1)}, bf16[2,192,8,512]{3,1,2,0:T(8,128)(2,1)S(1)}, u32[]{:S(2)}, u32[]{:S(2)}) collective-permute-start(bf16[2,192,8,512]{3,1,2,0:T(8,128)(2,1)S(1)} %pad_maximum_fusion), channel_id=1, source_target_pairs={{0,1},{1,2},{2,3},{3,4},{4,5},{5,6},{6,7},{7,8},{8,9},{9,10},{10,1... | collective-permute-start | bytes 9437192 | tf_op jit(solution)/shard_map/ppermute | solution.py:21
  105.0 1.6 copy-start.9
  106.6 51.2 %collective-permute-start.1 = (bf16[2,192,8,512]{3,1,2,0:T(8,128)(2,1)S(1)}, bf16[2,192,8,512]{3,1,2,0:T(8,128)(2,1)}, u32[]{:S(2)}, u32[]{:S(2)}) collective-permute-start(bf16[2,192,8,512]{3,1,2,0:T(8,128)(2,1)S(1)} %collective-permute-done), channel_id=1, source_target_pairs={{0,1},{1,2},{2,3},{3,4},{4,5},{5,6},{6,7},{7,8},{8,9},{9,10},{10,1... | collective-permute-start | bytes 9437192 | tf_op jit(solution)/shard_map/ppermute | solution.py:21
  157.9 43.6 %collective-permute-start.2 = (bf16[2,192,8,512]{3,1,2,0:T(8,128)(2,1)}, bf16[2,192,8,512]{3,1,2,0:T(8,128)(2,1)}, u32[]{:S(2)}, u32[]{:S(2)}) collective-permute-start(bf16[2,192,8,512]{3,1,2,0:T(8,128)(2,1)} %collective-permute-done.1), channel_id=1, source_target_pairs={{0,1},{1,2},{2,3},{3,4},{4,5},{5,6},{6,7},{7,8},{8,9},{9,10},{10,1... | collective-permute-start | bytes 9437192 | tf_op jit(solution)/shard_map/ppermute | solution.py:21
  201.5 440.8 %collective-permute-start.3 = (bf16[2,192,8,512]{3,1,2,0:T(8,128)(2,1)}, bf16[2,192,8,512]{3,1,2,0:T(8,128)(2,1)}, u32[]{:S(2)}, u32[]{:S(2)}) collective-permute-start(bf16[2,192,8,512]{3,1,2,0:T(8,128)(2,1)} %collective-permute-done.2), channel_id=1, source_target_pairs={{0,1},{1,2},{2,3},{3,4},{4,5},{5,6},{6,7},{7,8},{8,9},{9,10},{10,1... | collective-permute-start | bytes 9437192 | tf_op jit(solution)/shard_map/ppermute | solution.py:21
  527.9 5.8 copy-start
  535.0 1.9 copy-start.8
  577.3 8.7 %slice-start = ((s8[8388608]{0:T(1024)(128)(4,1)}), s8[4194304]{0:T(1024)(128)(4,1)S(1)}, s32[]{:S(2)}) async-start(s8[8388608]{0:T(1024)(128)(4,1)} %bitcast.160), calls=%async_computation.1 | async-start | bytes 8388608
  581.7 4.6 slice-start.1
  592.4 2.0 copy-start.6
  642.3 40.4 %collective-permute-start.4 = (bf16[2,192,8,512]{3,1,2,0:T(8,128)(2,1)}, bf16[2,192,8,512]{3,1,2,0:T(8,128)(2,1)}, u32[]{:S(2)}, u32[]{:S(2)}) collective-permute-start(bf16[2,192,8,512]{3,1,2,0:T(8,128)(2,1)} %collective-permute-done.3), channel_id=1, source_target_pairs={{0,1},{1,2},{2,3},{3,4},{4,5},{5,6},{6,7},{7,8},{8,9},{9,10},{10,1... | collective-permute-start | bytes 9437192 | tf_op jit(solution)/shard_map/ppermute | solution.py:21
  682.7 10.4 %copy-start.12 = (f32[8]{0:T(128)S(1)}, f32[8]{0:T(128)}, u32[]{:S(2)}) copy-start(f32[8]{0:T(128)} %param.15) | copy-start | bytes 100
  682.7 37.7 %collective-permute-start.5 = (bf16[2,192,8,512]{3,1,2,0:T(8,128)(2,1)}, bf16[2,192,8,512]{3,1,2,0:T(8,128)(2,1)}, u32[]{:S(2)}, u32[]{:S(2)}) collective-permute-start(bf16[2,192,8,512]{3,1,2,0:T(8,128)(2,1)} %collective-permute-done.4), channel_id=1, source_target_pairs={{0,1},{1,2},{2,3},{3,4},{4,5},{5,6},{6,7},{7,8},{8,9},{9,10},{10,1... | collective-permute-start | bytes 9437192 | tf_op jit(solution)/shard_map/ppermute | solution.py:21
  735.6 4.0 copy-start.10
Sparse Core Ops, SparseCore 0:
  34.6 493.2 all-reduce.2
where the time goes:
time: 789 us; the launch traced here: 781 us
  waiting for transfers between devices  478 us (61%)
  matrix products  183 us (23%)
  local copies, waits for them, and re-layouts  45.8 us (6%)
  other arithmetic  33.3 us (4%)
  starting transfers between devices  26.2 us (3%)
  between operations  14.5 us (2%)
    psum x1, waiting for transfers between devices, orthogonalize(): summed = lax.psum((gradient_one, gradient_three, gradient_two), 'ctx')  322 us
    ppermute x6, waiting for transfers between devices, passed_along(): return lax.ppermute(x, axis, pairs)  156 us
    dot_general x6, matrix products, mix_rows(): jnp.einsum('hrs,hsc->hrc', mixer, whole_matrix, preferred_element_type=jn...  83.6 us
    dot_general x6, matrix products, gram_of(): jnp.einsum('hrc,hsc->hrs', piece_rows, whole_matrix, preferred_element_ty...  40.3 us
    unnamed x40, local copies, waits for them, and re-layouts  40.3 us
    ppermute x6, starting transfers between devices, passed_along(): return lax.ppermute(x, axis, pairs)  26.1 us
  transfers between devices with their start and end apart: 7, of which 5 were waited for; matrix products, arithmetic and copies ran while one was open for 22% of the time, Pallas kernels for 0%

commit v1 on v0

v1 whole, which is shorter than its diff:
```python
import functools

import jax
import jax.numpy as jnp
from jax import lax
from jax.experimental import pallas as pl
from jax.experimental.pallas import tpu as pltpu
from jax.sharding import Mesh
from jax.sharding import PartitionSpec as P

WINDOW = 1024
NS_STEPS = 2

COEF_A = 3.4445
COEF_B = -4.775
COEF_C = 2.0315
EPSILON = 1e-06


def rms_heads(block):
    return block / jnp.sqrt(jnp.mean(block * block, axis=-1, keepdims=True) + EPSILON)


def to_heads(rows):
    return lax.all_to_all(rows, "mem", split_axis=1, concat_axis=0, tiled=True)


def to_tokens(rows):
    return lax.all_to_all(rows, "mem", split_axis=0, concat_axis=1, tiled=True)


def with_earlier(rows):
    tokens, groups = rows.shape[0], lax.axis_size("grp")
    parts, missing, distance = [rows], WINDOW, 1
    while missing > 0:
        take = min(missing, tokens)
        pairs = [(i, i + distance) for i in range(groups - distance)]
        parts.insert(0, lax.ppermute(rows[tokens - take :], "grp", pairs))
        missing -= take
        distance += 1
    return jnp.concatenate(parts, axis=0)


def window_attention(q, k, v):
    tokens, width = q.shape
    block = 512 if tokens % 512 == 0 else tokens
    count = tokens // block
    keys, values = with_earlier(k), with_earlier(v)
    reach = WINDOW + block
    keys = jnp.stack([keys[i * block : i * block + reach] for i in range(count)])
    values = jnp.stack([values[i * block : i * block + reach] for i in range(count)])
    scores = jnp.einsum(
        "bqd,bkd->bqk", q.reshape(count, block, width), keys, preferred_element_type=jnp.float32
    ) * width ** (-0.5)
    query_pos = lax.broadcasted_iota(jnp.int32, (count, block, reach), 1) + WINDOW
    key_pos = lax.broadcasted_iota(jnp.int32, (count, block, reach), 2)
    base = lax.broadcasted_iota(jnp.int32, (count, block, reach), 0) * block
    first_key = lax.axis_index("grp") * tokens - WINDOW
    offset = query_pos - key_pos
    allowed = (offset >= 0) & (offset < WINDOW) & (key_pos + base + first_key >= 0)
    scores = jnp.where(allowed, scores, -1e30)
    row_top = jnp.max(scores, axis=-1, keepdims=True)
    exponent = jnp.exp(scores - row_top)
    weights = (exponent / jnp.sum(exponent, axis=-1, keepdims=True)).astype(jnp.bfloat16)
    out = jnp.einsum("bqk,bkd->bqd", weights, values, preferred_element_type=jnp.float32)
    return out.reshape(tokens, width)


def orthogonal(gradient):
    squares = jnp.sum(gradient * gradient)
    current = (gradient / (jnp.sqrt(squares) + 1e-07)).astype(jnp.bfloat16)
    for sweep_index in range(NS_STEPS):
        gram = jnp.einsum(
            "rc,sc->rs", current, current, preferred_element_type=jnp.float32
        ).astype(jnp.bfloat16)
        mixer = (
            COEF_B * gram.astype(jnp.float32)
            + COEF_C * jnp.dot(gram, gram, preferred_element_type=jnp.float32)
        ).astype(jnp.bfloat16)
        current = (
            COEF_A * current.astype(jnp.float32)
            + jnp.dot(mixer, current, preferred_element_type=jnp.float32)
        ).astype(jnp.bfloat16)
    return current


def fast_weights(q, k, v, rates, one, three, two):
    f32 = jnp.float32
    key_normed = rms_heads(k.astype(f32)).astype(jnp.bfloat16)
    query_normed = rms_heads(q.astype(f32)).astype(jnp.bfloat16)
    hidden_one = jnp.dot(key_normed, one, preferred_element_type=f32)
    hidden_three = jnp.dot(key_normed, three, preferred_element_type=f32)
    sigmoid_one = jax.nn.sigmoid(hidden_one)
    active = hidden_one * sigmoid_one
    hidden = (active * hidden_three).astype(jnp.bfloat16)
    delta_out = (-rates * v.astype(f32)).astype(jnp.bfloat16)
    delta_hidden = jnp.einsum("td,fd->tf", delta_out, two, preferred_element_type=f32)
    delta_three = (delta_hidden * active).astype(jnp.bfloat16)
    delta_one = (
        delta_hidden * hidden_three * sigmoid_one * (1.0 + hidden_one * (1.0 - sigmoid_one))
    ).astype(jnp.bfloat16)
    gradient_one = jnp.einsum("td,tf->df", key_normed, delta_one, preferred_element_type=f32)
    gradient_three = jnp.einsum("td,tf->df", key_normed, delta_three, preferred_element_type=f32)
    gradient_two = jnp.einsum("tf,td->fd", hidden, delta_out, preferred_element_type=f32)
    grads = lax.psum(jnp.stack([gradient_one, gradient_three, gradient_two]), "grp")
    new = [
        (old.astype(f32) - orthogonal(grads[i]).astype(f32)).astype(jnp.bfloat16)
        for i, old in enumerate((one, three, two))
    ]
    query_one = jnp.dot(query_normed, new[0], preferred_element_type=f32)
    query_three = jnp.dot(query_normed, new[1], preferred_element_type=f32)
    query_hidden = (jax.nn.silu(query_one) * query_three).astype(jnp.bfloat16)
    return jnp.dot(query_hidden, new[2], preferred_element_type=f32)


def normed(rows):
    rows = rows.astype(jnp.float32)
    heads = lax.axis_size("head")
    total = lax.psum(jnp.sum(rows * rows, axis=1, keepdims=True), "head")
    return (rows / jnp.sqrt(total / (rows.shape[1] * heads) + EPSILON)).astype(jnp.bfloat16)


def local(queries, key_rows, value_rows, token_rates, fast_one, fast_three, fast_two, head_gain):
    me = lax.axis_index("mem")
    k, v, q = to_heads(key_rows), to_heads(value_rows), to_heads(queries)
    first = lax.axis_index("head") * head_gain.shape[0] if token_rates.shape[1] != head_gain.shape[0] else 0
    rates = lax.all_gather(token_rates, "mem", axis=0, tiled=True)
    rates = lax.dynamic_slice_in_dim(rates, me + first, 1, axis=1)
    one, three, two = (
        lax.dynamic_index_in_dim(w, me, 0, keepdims=False) for w in (fast_one, fast_three, fast_two)
    )
    gain = lax.dynamic_index_in_dim(head_gain, me, 0, keepdims=False)
    attended = window_attention(q, k, v)
    fast = fast_weights(q, k, v, rates, one, three, two) * gain
    window_rows = to_tokens(attended.astype(jnp.bfloat16))
    fast_rows = to_tokens(fast.astype(jnp.bfloat16))
    return normed(window_rows), normed(fast_rows)


def dot_nn(a, b):
    return jnp.dot(a, b, preferred_element_type=jnp.float32)


def dot_nt(a, b):
    return lax.dot_general(a, b, (((1,), (1,)), ((), ())), preferred_element_type=jnp.float32)


def dot_tn(a, b):
    return lax.dot_general(a, b, (((0,), (0,)), ((), ())), preferred_element_type=jnp.float32)


def layer_kernel(
    dims, k_hbm, v_hbm, q_hbm, rates_hbm, one_hbm, three_hbm, two_hbm, gain_ref,
    window_ref, fast_ref,
    kbuf, vbuf, qbuf, rbuf, weights, updated, grads, from_outer, from_inner, to_inner, to_outer,
    window_send, fast_send, window_recv, fast_recv,
    k_s, k_r, v_s, v_r, q_s, q_r, r_s, r_r, halo_s, halo_r, outer_r, inner_r, inner_s, outer_s,
    win_s, win_r, fast_s, fast_r, load_sem,
):
    groups, members, rows, width, pad, chunk = dims
    f32, bf16 = jnp.float32, jnp.bfloat16
    me, grp = lax.axis_index("mem"), lax.axis_index("grp")
    base = pad + WINDOW
    reach = base + rows
    stretch = members * rows
    chunks = 3 * width // chunk
    halo_first = (stretch - WINDOW) // rows
    halo_part = (halo_first + 1) * rows - (stretch - WINDOW)
    has_lower, has_upper = grp > 0, grp < groups - 1
    has_outer = jnp.logical_and(has_lower, has_upper)
    in_lower = grp < groups // 2
    inner = jnp.where(in_lower, grp + 1, grp - 1)
    outer = jnp.where(in_lower, grp - 1, grp + 1)
    is_mid = jnp.logical_or(grp == groups // 2 - 1, grp == groups // 2)

    barrier = pltpu.get_barrier_semaphore()
    for d in range(1, members):
        pl.semaphore_signal(barrier, inc=1, device_id={"mem": lax.rem(me + d, members)})

    @pl.when(has_lower)
    def _():
        pl.semaphore_signal(barrier, inc=1, device_id={"grp": grp - 1})

    @pl.when(has_upper)
    def _():
        pl.semaphore_signal(barrier, inc=1, device_id={"grp": grp + 1})

    pl.semaphore_wait(
        barrier, members - 1 + jnp.minimum(grp, 1) + jnp.minimum(groups - 1 - grp, 1)
    )

    def cols(p):
        return pl.ds(pl.multiple_of(p * width, width), width)

    def own_rows(s, first=base):
        return pl.ds(pl.multiple_of(first + s * rows, 16), rows)

    def exchange(hbm, buf, first, send, recv, d):
        peer = lax.rem(me + d, members)
        return pltpu.make_async_remote_copy(
            src_ref=hbm.at[:, cols(peer)], dst_ref=buf.at[own_rows(me, first)],
            send_sem=send.at[d], recv_sem=recv.at[d], device_id={"mem": peer},
        )

    def kept(hbm, buf, first, recv):
        return pltpu.make_async_copy(
            hbm.at[:, cols(me)], buf.at[own_rows(me, first)], recv.at[0]
        )

    def rates_to(d):
        peer = lax.rem(me + d, members)
        return pltpu.make_async_remote_copy(
            src_ref=rates_hbm.at[peer], dst_ref=rbuf.at[me],
            send_sem=r_s.at[d], recv_sem=r_r.at[d], device_id={"mem": peer},
        )

    def block_to(send_buf, recv_buf, send, recv, s):
        d = lax.rem(s - me + members, members)
        return pltpu.make_async_remote_copy(
            src_ref=send_buf.at[s], dst_ref=recv_buf.at[me],
            send_sem=send.at[d], recv_sem=recv.at[d], device_id={"mem": s},
        )

    own_rates = pltpu.make_async_copy(rates_hbm.at[me], rbuf.at[me], r_r.at[0])
    own_rates.start()
    kept(k_hbm, kbuf, base, k_r).start()
    kept(v_hbm, vbuf, base, v_r).start()
    kept(q_hbm, qbuf, 0, q_r).start()

    @pl.loop(1, members)
    def _(d):
        rates_to(d).start()
        exchange(k_hbm, kbuf, base, k_s, k_r, d).start()
        exchange(v_hbm, vbuf, base, v_s, v_r, d).start()

    loads = [
        pltpu.make_async_copy(hbm.at[me], weights.at[i], load_sem.at[i])
        for i, hbm in enumerate((one_hbm, three_hbm, two_hbm))
    ]
    for load in loads:
        load.start()
    kbuf[0:pad] = jnp.zeros((pad, width), bf16)
    vbuf[0:pad] = jnp.zeros((pad, width), bf16)

    @pl.when(grp == 0)
    def _():
        kbuf[pad:base] = jnp.zeros((WINDOW, width), bf16)
        vbuf[pad:base] = jnp.zeros((WINDOW, width), bf16)

    grads[...] = jnp.zeros_like(grads)
    for load in loads:
        load.wait()

    def halo_copies(s, size):
        start = base + s * rows + rows - size
        return [
            pltpu.make_async_remote_copy(
                src_ref=buf.at[pl.ds(pl.multiple_of(start, 16), size)],
                dst_ref=buf.at[pl.ds(pl.multiple_of(start - stretch, 16), size)],
                send_sem=halo_s.at[i, s], recv_sem=halo_r.at[i, s], device_id={"grp": grp + 1},
            )
            for i, buf in enumerate((kbuf, vbuf))
        ]

    def for_halo(s, present, act):
        @pl.when(jnp.logical_and(present, s == halo_first))
        def _():
            for copy in halo_copies(s, halo_part):
                act(copy)

        @pl.when(jnp.logical_and(present, s > halo_first))
        def _():
            for copy in halo_copies(s, rows):
                act(copy)

    def rms_unit(x):
        x = x.astype(f32)
        return (x * lax.rsqrt(jnp.mean(x * x, axis=1, keepdims=True) + EPSILON)).astype(bf16)

    @pl.loop(0, members)
    def _(d):
        s = lax.rem(me - d + members, members)

        @pl.when(d == 0)
        def _():
            own_rates.wait()
            kept(k_hbm, kbuf, base, k_r).wait()
            kept(v_hbm, vbuf, base, v_r).wait()

        @pl.when(d > 0)
        def _():
            rates_to(d).wait_recv()
            exchange(k_hbm, kbuf, base, k_s, k_r, d).wait_recv()
            exchange(v_hbm, vbuf, base, v_s, v_r, d).wait_recv()

        for_halo(s, has_upper, lambda copy: copy.start())

        @pl.when(d == members // 2)
        def _():
            @pl.loop(1, members)
            def _(e):
                exchange(q_hbm, qbuf, 0, q_s, q_r, e).start()

        key_unit = rms_unit(kbuf[own_rows(s)])
        rate_row = rbuf[s][0:1]
        lanes = rate_row.shape[1]
        diagonal = lax.broadcasted_iota(jnp.int32, (rows, lanes), 0) == lax.broadcasted_iota(
            jnp.int32, (rows, lanes), 1
        )
        rate = jnp.sum(jnp.where(diagonal, rate_row, 0.0), axis=1, keepdims=True)
        delta_out = (-rate * vbuf[own_rows(s)].astype(f32)).astype(bf16)
        a = dot_nn(key_unit, weights[0])
        b = dot_nn(key_unit, weights[1])
        dh = dot_nt(delta_out, weights[2])
        sig = 1.0 / (1.0 + jnp.exp(-a))
        active = a * sig
        hidden = (active * b).astype(bf16)
        delta_three = (dh * active).astype(bf16)
        delta_one = (dh * b * sig * (1.0 + a * (1.0 - sig))).astype(bf16)
        grads[0:width] += dot_tn(key_unit, delta_one)
        grads[width : 2 * width] += dot_tn(key_unit, delta_three)
        grads[2 * width : 3 * width] += dot_tn(hidden, delta_out)

    def rows_of(i):
        return pl.ds(pl.multiple_of(i * chunk, chunk), chunk)

    def inward(i, target, recv):
        return pltpu.make_async_remote_copy(
            src_ref=to_inner.at[i], dst_ref=target.at[i],
            send_sem=inner_s.at[i], recv_sem=recv.at[i], device_id={"grp": inner},
        )

    def outward(i):
        return pltpu.make_async_remote_copy(
            src_ref=to_outer.at[i], dst_ref=from_inner.at[i],
            send_sem=outer_s.at[i], recv_sem=inner_r.at[i], device_id={"grp": outer},
        )

    def send_inward(i):
        @pl.when(is_mid)
        def _():
            inward(i, from_inner, inner_r).start()

        @pl.when(jnp.logical_not(is_mid))
        def _():
            inward(i, from_outer, outer_r).start()

    @pl.when(jnp.logical_not(has_outer))
    def _():
        @pl.loop(0, chunks)
        def _(i):
            to_inner[i] = grads[rows_of(i)].astype(bf16)
            send_inward(i)

    def attend(s):
        scores = dot_nt(qbuf[own_rows(s, 0)], kbuf[pl.ds(pl.multiple_of(s * rows, 16), reach)])
        scores = scores * width ** (-0.5)
        query = lax.broadcasted_iota(jnp.int32, (rows, reach), 0)
        key = lax.broadcasted_iota(jnp.int32, (rows, reach), 1)
        offset = query - key + base
        first = grp * stretch + s * rows - base
        allowed = (offset >= 0) & (offset < WINDOW) & (key + first >= 0)
        scores = jnp.where(allowed, scores, -1e30)
        top = jnp.max(scores, axis=1, keepdims=True)
        exponent = jnp.exp(scores - top)
        total = jnp.sum(exponent, axis=1, keepdims=True)
        out = dot_nn(
            exponent.astype(bf16), vbuf[pl.ds(pl.multiple_of(s * rows, 16), reach)]
        )
        return (out / total).astype(bf16)

    lag = 2

    @pl.loop(0, chunks + lag)
    def _(i):
        @pl.when(jnp.logical_and(has_outer, i < chunks))
        def _():
            inward(i, from_outer, outer_r).wait_recv()
            partial = grads[rows_of(i)] + from_outer[i].astype(f32)
            to_inner[i] = partial.astype(bf16)
            send_inward(i)

        @pl.when(i >= lag)
        def _():
            j = i - lag
            outward(j).wait_recv()

            @pl.when(is_mid)
            def _():
                grads[rows_of(j)] = to_inner[j].astype(f32) + from_inner[j].astype(f32)

            @pl.when(jnp.logical_not(is_mid))
            def _():
                grads[rows_of(j)] = from_inner[j].astype(f32)

            @pl.when(has_outer)
            def _():
                to_outer[j] = grads[rows_of(j)].astype(bf16)
                outward(j).start()

        @pl.when(jnp.logical_and(i >= chunks - members, i < chunks))
        def _():
            s = chunks - 1 - i
            d = lax.rem(me - s + members, members)

            @pl.when(d == 0)
            def _():
                kept(q_hbm, qbuf, 0, q_r).wait()

            @pl.when(d > 0)
            def _():
                exchange(q_hbm, qbuf, 0, q_s, q_r, d).wait_recv()

            piece = s + halo_first
            for_halo(
                piece, jnp.logical_and(has_lower, piece < members), lambda copy: copy.wait_recv()
            )
            block = attend(s)

            @pl.when(s == me)
            def _():
                window_recv[s] = block

            @pl.when(s != me)
            def _():
                window_send[s] = block
                block_to(window_send, window_recv, win_s, win_r, s).start()

    @pl.loop(0, 3)
    def _(m):
        gradient = grads[pl.ds(pl.multiple_of(m * width, width), width)]
        squares = jnp.sum(jnp.sum(gradient * gradient, axis=1, keepdims=True), axis=0, keepdims=True)
        current = (gradient / (jnp.sqrt(squares) + 1e-07)).astype(bf16)
        for sweep_index in range(NS_STEPS):
            gram = dot_nt(current, current).astype(bf16)
            mixer = (COEF_B * gram.astype(f32) + COEF_C * dot_nn(gram, gram)).astype(bf16)
            current = (COEF_A * current.astype(f32) + dot_nn(mixer, current)).astype(bf16)
        updated[m] = (weights[m].astype(f32) - current.astype(f32)).astype(bf16)

    gain = gain_ref[me]

    @pl.loop(1, members + 1)
    def _(d):
        s = lax.rem(me + d, members)
        unit = rms_unit(qbuf[own_rows(s, 0)])
        a = dot_nn(unit, updated[0])
        b = dot_nn(unit, updated[1])
        hidden = (a / (1.0 + jnp.exp(-a)) * b).astype(bf16)
        block = (dot_nn(hidden, updated[2]) * gain).astype(bf16)

        @pl.when(s == me)
        def _():
            fast_recv[s] = block

        @pl.when(s != me)
        def _():
            fast_send[s] = block
            block_to(fast_send, fast_recv, fast_s, fast_r, s).start()

    def finish(recv, out):
        total = jnp.zeros((rows, 1), f32)
        for h in range(members):
            x = recv[h].astype(f32)
            total = total + jnp.sum(x * x, axis=1, keepdims=True)
        scale = lax.rsqrt(total / (members * width) + EPSILON)
        for h in range(members):
            out[:, h * width : (h + 1) * width] = (recv[h].astype(f32) * scale).astype(bf16)

    def arrivals(send_buf, recv_buf, send, recv):
        @pl.loop(1, members)
        def _(d):
            block_to(send_buf, recv_buf, send, recv, lax.rem(me + d, members)).wait_recv()

    arrivals(window_send, window_recv, win_s, win_r)
    finish(window_recv, window_ref)
    arrivals(fast_send, fast_recv, fast_s, fast_r)
    finish(fast_recv, fast_ref)

    @pl.loop(1, members)
    def _(d):
        s = lax.rem(me + d, members)
        rates_to(d).wait_send()
        exchange(k_hbm, kbuf, base, k_s, k_r, d).wait_send()
        exchange(v_hbm, vbuf, base, v_s, v_r, d).wait_send()
        exchange(q_hbm, qbuf, 0, q_s, q_r, d).wait_send()
        block_to(window_send, window_recv, win_s, win_r, s).wait_send()
        block_to(fast_send, fast_recv, fast_s, fast_r, s).wait_send()

    @pl.loop(0, members)
    def _(s):
        for_halo(s, has_upper, lambda copy: copy.wait_send())

    @pl.loop(0, chunks)
    def _(i):
        inward(i, from_inner, inner_r).wait_send()

        @pl.when(has_outer)
        def _():
            outward(i).wait_send()


def local_kernel(queries, key_rows, value_rows, token_rates, fast_one, fast_three, fast_two, head_gain):
    groups, members = lax.axis_size("grp"), lax.axis_size("mem")
    rows, width = queries.shape[0], fast_one.shape[1]
    pad = -(WINDOW + rows) % 128
    chunk = 128
    chunks = 3 * width // chunk
    lanes = rows + -rows % 128
    rates = jnp.pad(token_rates.T, ((0, 0), (0, lanes - rows)))
    rates = jnp.broadcast_to(rates[:, None, :], (members, 8, lanes))
    bf16, dma = jnp.bfloat16, pltpu.SemaphoreType.DMA
    keys = pltpu.VMEM((pad + WINDOW + members * rows, width), bf16)
    parts = pltpu.VMEM((chunks, chunk, width), bf16)
    blocks = pltpu.VMEM((members, rows, width), bf16)
    matrices = pltpu.VMEM((3, width, width), bf16)
    anywhere, vmem = pl.BlockSpec(memory_space=pl.ANY), pl.BlockSpec(memory_space=pltpu.VMEM)
    out = jax.ShapeDtypeStruct(queries.shape, bf16)
    return pl.pallas_call(
        functools.partial(layer_kernel, (groups, members, rows, width, pad, chunk)),
        out_shape=(out, out),
        in_specs=[anywhere] * 7 + [pl.BlockSpec(memory_space=pltpu.SMEM)],
        out_specs=(vmem, vmem),
        scratch_shapes=[
            keys, keys, pltpu.VMEM((members * rows, width), bf16),
            pltpu.VMEM((members, 8, lanes), jnp.float32),
            matrices, matrices, pltpu.VMEM((3 * width, width), jnp.float32),
            parts, parts, parts, parts, blocks, blocks, blocks, blocks,
        ]
        + [dma((members,))] * 8
        + [dma((2, members))] * 2
        + [dma((chunks,))] * 4
        + [dma((members,))] * 4
        + [dma((3,))],
        compiler_params=pltpu.CompilerParams(
            collective_id=0, has_side_effects=True, vmem_limit_bytes=56 * 2**20
        ),
        cost_estimate=pl.CostEstimate(
            flops=16 * 2**30, bytes_accessed=10 * 2**20, transcendentals=4 * 2**20
        ),
    )(key_rows, value_rows, queries, rates, fast_one, fast_three, fast_two, head_gain)


def solution(mesh):
    ctx, head = mesh.shape["ctx"], mesh.shape["head"]
    def run(*args):
        members = args[4].shape[0] // head
        split = Mesh(mesh.devices.reshape(ctx // members, members, head), ("grp", "mem", "head"))
        rows = P(("grp", "mem"), "head")
        weights = P("head", None, None)
        groups, width, rows_here = ctx // members, args[4].shape[1], args[0].shape[0] // ctx
        whole_blocks = rows_here % 64 == 0 and width % 128 == 0 and members * rows_here > WINDOW
        fits = whole_blocks and members > 1 and groups % 2 == 0 and 3 * width // 128 >= members
        return jax.shard_map(
            local_kernel if fits and head == 1 else local,
            mesh=split,
            in_specs=(rows, rows, rows, rows, weights, weights, weights, P("head")),
            out_specs=(rows, rows),
            check_vma=False,
        )(*args)

    return run
```

time: 789 us -> 138 us (0.17); the launches traced: 781 us -> 138 us
  waiting for transfers between devices: 478 us -> 0 us
  matrix products: 183 us -> 0 us
  Pallas kernels: 0 us -> 132 us
  local copies, waits for them, and re-layouts: 45.8 us -> 5.31 us
  other arithmetic: 33.3 us -> 0 us
  starting transfers between devices: 26.2 us -> 0 us
  between operations: 14.5 us -> 0.65 us
    psum x1 -> x0, waiting for transfers between devices: 322 us -> none  [orthogonalize(): summed = lax.psum((gradient_one, gradient_three, gradient_two), 'ctx')]
    dot_general x22 -> x0, matrix products: 183 us -> none  [the longest x6 83.6 us: mix_rows(): jnp.einsum('hrs,hsc->hrc', mixer, whole_matrix, preferred_element_type=jn...]
    ppermute x6 -> x0, waiting for transfers between devices: 156 us -> none  [passed_along(): return lax.ppermute(x, axis, pairs)]
    pallas_call x0 -> x1, Pallas kernels: none -> 132 us  [local_kernel(): pl.pallas_call(functools.partial(layer_kernel, (groups, members, rows, wi...]
    unnamed x40 -> x4, local copies, waits for them, and re-layouts: 40.3 us -> 3.97 us
    ppermute x6 -> x0, starting transfers between devices: 26.1 us -> none  [passed_along(): return lax.ppermute(x, axis, pairs)]
    reduce_sum x5 -> x0, other arithmetic: 15.2 us -> none  [the longest x3 13.1 us: orthogonalize(): jnp.sum(matrix * matrix, axis=(1, 2))]
    convert_element_type x4 -> x0, other arithmetic: 8.09 us -> none  [the longest x2 7.47 us: start_iterate(): (gradient / (jnp.sqrt(squares)[:, None, None] + 1e-07)).astype(jnp.bfloat16)]
  transfers between devices with their start and end apart: 7 -> 0, of which waited for: 5 -> 0; matrix products, arithmetic and copies ran while one was open for 22% -> 0% of each run, Pallas kernels for 0% -> 0%
where the time goes in v1:
time: 138 us
  Pallas kernels  132 us (96%)
  local copies, waits for them, and re-layouts  5.31 us (4%)
    pallas_call x1, Pallas kernels, local_kernel(): pl.pallas_call(functools.partial(layer_kernel, (groups, members, rows, wi...  132 us
    unnamed x4, local copies, waits for them, and re-layouts  3.97 us

profile of v1, /device:TPU:1, one launch (start us, length us, event | category | flops | bytes accessed | tf_op | source)
XLA Modules:
  0.0 138.0 jit_solution(7118666574747814851)
XLA Ops:
  0.6 0.7 pad.4
  1.3 0.6 broadcast_in_dim.2.rates_hbm
  2.0 132.0 %shard_map.95 = (bf16[192,4096]{1,0:T(8,128)(2,1)}, bf16[192,4096]{1,0:T(8,128)(2,1)}) custom-call(bf16[192,4096]{1,0:T(8,128)(2,1)} %k_hbm.1, bf16[192,4096]{1,0:T(8,128)(2,1)} %v_hbm.1, bf16[192,4096]{1,0:T(8,128)(2,1)} %q_hbm.1, f32[8,8,256]{2,1,0:T(8,128)} %broadcast_in_dim.2.rates_hbm, bf16[8,512,512]{2,1,0:T(8,128)(2,1)} %one_hbm.1, ...), custom_call_target="tpu_custom_call" | custom-call | flops 17179869184 | bytes 10485760 | tf_op jit(solution)/shard_map/pallas_call | solution.py:518
  134.0 0.0 copy-start
  134.0 2.8 %copy.12 = bf16[192,4096]{1,0:T(8,128)(2,1)} copy(bf16[192,4096]{1,0:T(8,128)(2,1)} %get-tuple-element.4) | data formatting | bytes 3145728
  136.8 0.0 copy-done
  136.8 1.1 copy.13
Async XLA Ops:
  134.0 2.8 %copy-start = (bf16[192,4096]{1,0:T(8,128)(2,1)S(1)}, bf16[192,4096]{1,0:T(8,128)(2,1)}, u32[]{:S(2)}) copy-start(bf16[192,4096]{1,0:T(8,128)(2,1)} %get-tuple-element.5) | copy-start | bytes 4718596

commit v2 on v1

--- a/solution.py
+++ b/solution.py
@@ -149,11 +149,19 @@
     return lax.dot_general(a, b, (((0,), (0,)), ((), ())), preferred_element_type=jnp.float32)
 
 
+def other_member(a, b, count):
+    out, bit = 0, 1
+    while bit < count:
+        out = out + bit * lax.rem(a // bit + b // bit, 2)
+        bit *= 2
+    return out
+
+
 def layer_kernel(
     dims, k_hbm, v_hbm, q_hbm, rates_hbm, one_hbm, three_hbm, two_hbm, gain_ref,
-    window_ref, fast_ref,
+    window_recv, fast_recv,
     kbuf, vbuf, qbuf, rbuf, weights, updated, grads, from_outer, from_inner, to_inner, to_outer,
-    window_send, fast_send, window_recv, fast_recv,
+    window_send, fast_send,
     k_s, k_r, v_s, v_r, q_s, q_r, r_s, r_r, halo_s, halo_r, outer_r, inner_r, inner_s, outer_s,
     win_s, win_r, fast_s, fast_r, load_sem,
 ):
@@ -196,7 +204,7 @@
         return pl.ds(pl.multiple_of(first + s * rows, 16), rows)
 
     def exchange(hbm, buf, first, send, recv, d):
-        peer = lax.rem(me + d, members)
+        peer = other_member(me, d, members)
         return pltpu.make_async_remote_copy(
             src_ref=hbm.at[:, cols(peer)], dst_ref=buf.at[own_rows(me, first)],
             send_sem=send.at[d], recv_sem=recv.at[d], device_id={"mem": peer},
@@ -208,20 +216,23 @@
         )
 
     def rates_to(d):
-        peer = lax.rem(me + d, members)
+        peer = other_member(me, d, members)
         return pltpu.make_async_remote_copy(
-            src_ref=rates_hbm.at[peer], dst_ref=rbuf.at[me],
+            src_ref=rates_hbm, dst_ref=rbuf.at[me],
             send_sem=r_s.at[d], recv_sem=r_r.at[d], device_id={"mem": peer},
         )
 
     def block_to(send_buf, recv_buf, send, recv, s):
-        d = lax.rem(s - me + members, members)
+        d = other_member(me, s, members)
         return pltpu.make_async_remote_copy(
             src_ref=send_buf.at[s], dst_ref=recv_buf.at[me],
             send_sem=send.at[d], recv_sem=recv.at[d], device_id={"mem": s},
         )
 
-    own_rates = pltpu.make_async_copy(rates_hbm.at[me], rbuf.at[me], r_r.at[0])
+    def block_kept(send_buf, recv_buf, recv):
+        return pltpu.make_async_copy(send_buf.at[me], recv_buf.at[me], recv.at[0])
+
+    own_rates = pltpu.make_async_copy(rates_hbm, rbuf.at[me], r_r.at[0])
     own_rates.start()
     kept(k_hbm, kbuf, base, k_r).start()
     kept(v_hbm, vbuf, base, v_r).start()
@@ -229,9 +240,15 @@
 
     @pl.loop(1, members)
     def _(d):
+        exchange(k_hbm, kbuf, base, k_s, k_r, d).start()
+
+        @pl.when(d == 1)
+        def _():
+            exchange(v_hbm, vbuf, base, v_s, v_r, d).start()
+
+    @pl.loop(1, members)
+    def _(d):
         rates_to(d).start()
-        exchange(k_hbm, kbuf, base, k_s, k_r, d).start()
-        exchange(v_hbm, vbuf, base, v_s, v_r, d).start()
 
     loads = [
         pltpu.make_async_copy(hbm.at[me], weights.at[i], load_sem.at[i])
@@ -251,27 +268,24 @@
     for load in loads:
         load.wait()
 
-    def halo_copies(s, size):
+    def halo_copy(which, s, size):
+        buf = (kbuf, vbuf)[which]
         start = base + s * rows + rows - size
-        return [
-            pltpu.make_async_remote_copy(
-                src_ref=buf.at[pl.ds(pl.multiple_of(start, 16), size)],
-                dst_ref=buf.at[pl.ds(pl.multiple_of(start - stretch, 16), size)],
-                send_sem=halo_s.at[i, s], recv_sem=halo_r.at[i, s], device_id={"grp": grp + 1},
-            )
-            for i, buf in enumerate((kbuf, vbuf))
-        ]
-
-    def for_halo(s, present, act):
+        return pltpu.make_async_remote_copy(
+            src_ref=buf.at[pl.ds(pl.multiple_of(start, 16), size)],
+            dst_ref=buf.at[pl.ds(pl.multiple_of(start - stretch, 16), size)],
+            send_sem=halo_s.at[which, s], recv_sem=halo_r.at[which, s],
+            device_id={"grp": grp + 1},
+        )
+
+    def for_halo(which, s, present, act):
         @pl.when(jnp.logical_and(present, s == halo_first))
         def _():
-            for copy in halo_copies(s, halo_part):
-                act(copy)
+            act(halo_copy(which, s, halo_part))
 
         @pl.when(jnp.logical_and(present, s > halo_first))
         def _():
-            for copy in halo_copies(s, rows):
-                act(copy)
+            act(halo_copy(which, s, rows))
 
     def rms_unit(x):
         x = x.astype(f32)
@@ -279,33 +293,60 @@
 
     @pl.loop(0, members)
     def _(d):
-        s = lax.rem(me - d + members, members)
+        s = other_member(me, d, members)
 
         @pl.when(d == 0)
         def _():
+            kept(k_hbm, kbuf, base, k_r).wait()
+
+        @pl.when(d > 0)
+        def _():
+            exchange(k_hbm, kbuf, base, k_s, k_r, d).wait_recv()
+
+        for_halo(0, s, has_upper, lambda copy: copy.start())
+
+        @pl.when(d > 1)
+        def _():
+            exchange(v_hbm, vbuf, base, v_s, v_r, d).start()
+
+        @pl.when(d == 0)
+        def _():
+            kept(v_hbm, vbuf, base, v_r).wait()
+
+        @pl.when(d == 1)
+        def _():
+            exchange(v_hbm, vbuf, base, v_s, v_r, d).wait_recv()
+
+        for_halo(1, s, jnp.logical_and(has_upper, d < 2), lambda copy: copy.start())
+
+    @pl.loop(0, members)
+    def _(d):
+        s = other_member(me, d, members)
+
+        @pl.when(d == 0)
+        def _():
             own_rates.wait()
-            kept(k_hbm, kbuf, base, k_r).wait()
-            kept(v_hbm, vbuf, base, v_r).wait()
 
         @pl.when(d > 0)
         def _():
             rates_to(d).wait_recv()
-            exchange(k_hbm, kbuf, base, k_s, k_r, d).wait_recv()
+
+        @pl.when(d > 1)
+        def _():
             exchange(v_hbm, vbuf, base, v_s, v_r, d).wait_recv()
 
-        for_halo(s, has_upper, lambda copy: copy.start())
-
-        @pl.when(d == members // 2)
-        def _():
-            @pl.loop(1, members)
-            def _(e):
-                exchange(q_hbm, qbuf, 0, q_s, q_r, e).start()
+        for_halo(1, s, jnp.logical_and(has_upper, d > 1), lambda copy: copy.start())
+
+        @pl.when(d > 0)
+        def _():
+            exchange(q_hbm, qbuf, 0, q_s, q_r, d).start()
 
         key_unit = rms_unit(kbuf[own_rows(s)])
-        rate_row = rbuf[s][0:1]
-        lanes = rate_row.shape[1]
-        diagonal = lax.broadcasted_iota(jnp.int32, (rows, lanes), 0) == lax.broadcasted_iota(
-            jnp.int32, (rows, lanes), 1
+        heads_rates = rbuf[s]
+        is_mine = lax.broadcasted_iota(jnp.int32, heads_rates.shape, 0) == me
+        rate_row = jnp.sum(jnp.where(is_mine, heads_rates, 0.0), axis=0, keepdims=True)
+        diagonal = lax.broadcasted_iota(jnp.int32, (rows, rows), 0) == lax.broadcasted_iota(
+            jnp.int32, (rows, rows), 1
         )
         rate = jnp.sum(jnp.where(diagonal, rate_row, 0.0), axis=1, keepdims=True)
         delta_out = (-rate * vbuf[own_rows(s)].astype(f32)).astype(bf16)
@@ -369,65 +410,7 @@
         )
         return (out / total).astype(bf16)
 
-    lag = 2
-
-    @pl.loop(0, chunks + lag)
-    def _(i):
-        @pl.when(jnp.logical_and(has_outer, i < chunks))
-        def _():
-            inward(i, from_outer, outer_r).wait_recv()
-            partial = grads[rows_of(i)] + from_outer[i].astype(f32)
-            to_inner[i] = partial.astype(bf16)
-            send_inward(i)
-
-        @pl.when(i >= lag)
-        def _():
-            j = i - lag
-            outward(j).wait_recv()
-
-            @pl.when(is_mid)
-            def _():
-                grads[rows_of(j)] = to_inner[j].astype(f32) + from_inner[j].astype(f32)
-
-            @pl.when(jnp.logical_not(is_mid))
-            def _():
-                grads[rows_of(j)] = from_inner[j].astype(f32)
-
-            @pl.when(has_outer)
-            def _():
-                to_outer[j] = grads[rows_of(j)].astype(bf16)
-                outward(j).start()
-
-        @pl.when(jnp.logical_and(i >= chunks - members, i < chunks))
-        def _():
-            s = chunks - 1 - i
-            d = lax.rem(me - s + members, members)
-
-            @pl.when(d == 0)
-            def _():
-                kept(q_hbm, qbuf, 0, q_r).wait()
-
-            @pl.when(d > 0)
-            def _():
-                exchange(q_hbm, qbuf, 0, q_s, q_r, d).wait_recv()
-
-            piece = s + halo_first
-            for_halo(
-                piece, jnp.logical_and(has_lower, piece < members), lambda copy: copy.wait_recv()
-            )
-            block = attend(s)
-
-            @pl.when(s == me)
-            def _():
-                window_recv[s] = block
-
-            @pl.when(s != me)
-            def _():
-                window_send[s] = block
-                block_to(window_send, window_recv, win_s, win_r, s).start()
-
-    @pl.loop(0, 3)
-    def _(m):
+    def orthogonal_update(m):
         gradient = grads[pl.ds(pl.multiple_of(m * width, width), width)]
         squares = jnp.sum(jnp.sum(gradient * gradient, axis=1, keepdims=True), axis=0, keepdims=True)
         current = (gradient / (jnp.sqrt(squares) + 1e-07)).astype(bf16)
@@ -437,48 +420,100 @@
             current = (COEF_A * current.astype(f32) + dot_nn(mixer, current)).astype(bf16)
         updated[m] = (weights[m].astype(f32) - current.astype(f32)).astype(bf16)
 
+    per_matrix = width // chunk
+    lag = 2
+
+    @pl.loop(0, chunks + lag)
+    def _(i):
+        @pl.when(jnp.logical_and(has_outer, i < chunks))
+        def _():
+            inward(i, from_outer, outer_r).wait_recv()
+            partial = grads[rows_of(i)] + from_outer[i].astype(f32)
+            to_inner[i] = partial.astype(bf16)
+            send_inward(i)
+
+        @pl.when(i >= lag)
+        def _():
+            j = i - lag
+            outward(j).wait_recv()
+
+            @pl.when(is_mid)
+            def _():
+                grads[rows_of(j)] = to_inner[j].astype(f32) + from_inner[j].astype(f32)
+
+            @pl.when(jnp.logical_not(is_mid))
+            def _():
+                grads[rows_of(j)] = from_inner[j].astype(f32)
+
+            @pl.when(has_outer)
+            def _():
+                to_outer[j] = grads[rows_of(j)].astype(bf16)
+                outward(j).start()
+
+            @pl.when(lax.rem(j, per_matrix) == per_matrix - 1)
+            def _():
+                orthogonal_update(j // per_matrix)
+
+        @pl.when(jnp.logical_and(i >= chunks - members, i < chunks))
+        def _():
+            s = chunks - 1 - i
+            d = other_member(me, s, members)
+
+            @pl.when(d == 0)
+            def _():
+                kept(q_hbm, qbuf, 0, q_r).wait()
+
+            @pl.when(d > 0)
+            def _():
+                exchange(q_hbm, qbuf, 0, q_s, q_r, d).wait_recv()
+
+            piece = s + halo_first
+            for which in range(2):
+                for_halo(
+                    which, piece, jnp.logical_and(has_lower, piece < members),
+                    lambda copy: copy.wait_recv(),
+                )
+            window_send[s] = attend(s)
+
+            @pl.when(s == me)
+            def _():
+                block_kept(window_send, window_recv, win_r).start()
+
+            @pl.when(s != me)
+            def _():
+                block_to(window_send, window_recv, win_s, win_r, s).start()
+
     gain = gain_ref[me]
 
-    @pl.loop(1, members + 1)
+    @pl.loop(0, members)
     def _(d):
-        s = lax.rem(me + d, members)
+        s = other_member(me, members - 1 - d, members)
         unit = rms_unit(qbuf[own_rows(s, 0)])
         a = dot_nn(unit, updated[0])
         b = dot_nn(unit, updated[1])
         hidden = (a / (1.0 + jnp.exp(-a)) * b).astype(bf16)
-        block = (dot_nn(hidden, updated[2]) * gain).astype(bf16)
+        fast_send[s] = (dot_nn(hidden, updated[2]) * gain).astype(bf16)
 
         @pl.when(s == me)
         def _():
-            fast_recv[s] = block
+            block_kept(fast_send, fast_recv, fast_r).start()
 
         @pl.when(s != me)
         def _():
-            fast_send[s] = block
             block_to(fast_send, fast_recv, fast_s, fast_r, s).start()
 
-    def finish(recv, out):
-        total = jnp.zeros((rows, 1), f32)
-        for h in range(members):
-            x = recv[h].astype(f32)
-            total = total + jnp.sum(x * x, axis=1, keepdims=True)
-        scale = lax.rsqrt(total / (members * width) + EPSILON)
-        for h in range(members):
-            out[:, h * width : (h + 1) * width] = (recv[h].astype(f32) * scale).astype(bf16)
-
-    def arrivals(send_buf, recv_buf, send, recv):
-        @pl.loop(1, members)
-        def _(d):
-            block_to(send_buf, recv_buf, send, recv, lax.rem(me + d, members)).wait_recv()
-
-    arrivals(window_send, window_recv, win_s, win_r)
-    finish(window_recv, window_ref)
-    arrivals(fast_send, fast_recv, fast_s, fast_r)
-    finish(fast_recv, fast_ref)
+    block_kept(window_send, window_recv, win_r).wait()
+    block_kept(fast_send, fast_recv, fast_r).wait()
 
     @pl.loop(1, members)
     def _(d):
-        s = lax.rem(me + d, members)
+        s = other_member(me, d, members)
+        block_to(window_send, window_recv, win_s, win_r, s).wait_recv()
+        block_to(fast_send, fast_recv, fast_s, fast_r, s).wait_recv()
+
+    @pl.loop(1, members)
+    def _(d):
+        s = other_member(me, d, members)
         rates_to(d).wait_send()
         exchange(k_hbm, kbuf, base, k_s, k_r, d).wait_send()
         exchange(v_hbm, vbuf, base, v_s, v_r, d).wait_send()
@@ -488,7 +523,8 @@
 
     @pl.loop(0, members)
     def _(s):
-        for_halo(s, has_upper, lambda copy: copy.wait_send())
+        for which in range(2):
+            for_halo(which, s, has_upper, lambda copy: copy.wait_send())
 
     @pl.loop(0, chunks)
     def _(i):
@@ -497,6 +533,39 @@
         @pl.when(has_outer)
         def _():
             outward(i).wait_send()
+
+
+def norm_kernel(window_raw, fast_raw, window_ref, fast_ref):
+    heads, _, width = window_raw.shape
+    for raw, out in ((window_raw, window_ref), (fast_raw, fast_ref)):
+        total = 0.0
+        for h in range(heads):
+            x = raw[h].astype(jnp.float32)
+            total = total + jnp.sum(x * x, axis=1, keepdims=True)
+        scale = lax.rsqrt(total / (heads * width) + EPSILON)
+        for h in range(heads):
+            out[:, h * width : (h + 1) * width] = (raw[h].astype(jnp.float32) * scale).astype(
+                jnp.bfloat16
+            )
+
+
+def normed_rows(window_raw, fast_raw):
+    heads, rows, width = window_raw.shape
+    block = 64
+    raw = pl.BlockSpec((heads, block, width), lambda i: (0, i, 0))
+    done = pl.BlockSpec((block, heads * width), lambda i: (i, 0))
+    out = jax.ShapeDtypeStruct((rows, heads * width), jnp.bfloat16)
+    return pl.pallas_call(
+        norm_kernel,
+        grid=(rows // block,),
+        out_shape=(out, out),
+        in_specs=[raw, raw],
+        out_specs=(done, done),
+        compiler_params=pltpu.CompilerParams(vmem_limit_bytes=60 * 2**20),
+        cost_estimate=pl.CostEstimate(
+            flops=8 * rows * heads * width, bytes_accessed=8 * rows * heads * width, transcendentals=0
+        ),
+    )(window_raw, fast_raw)
 
 
 def local_kernel(queries, key_rows, value_rows, token_rates, fast_one, fast_three, fast_two, head_gain):
@@ -505,26 +574,23 @@
     pad = -(WINDOW + rows) % 128
     chunk = 128
     chunks = 3 * width // chunk
-    lanes = rows + -rows % 128
-    rates = jnp.pad(token_rates.T, ((0, 0), (0, lanes - rows)))
-    rates = jnp.broadcast_to(rates[:, None, :], (members, 8, lanes))
     bf16, dma = jnp.bfloat16, pltpu.SemaphoreType.DMA
     keys = pltpu.VMEM((pad + WINDOW + members * rows, width), bf16)
     parts = pltpu.VMEM((chunks, chunk, width), bf16)
     blocks = pltpu.VMEM((members, rows, width), bf16)
     matrices = pltpu.VMEM((3, width, width), bf16)
-    anywhere, vmem = pl.BlockSpec(memory_space=pl.ANY), pl.BlockSpec(memory_space=pltpu.VMEM)
-    out = jax.ShapeDtypeStruct(queries.shape, bf16)
-    return pl.pallas_call(
+    anywhere = pl.BlockSpec(memory_space=pl.ANY)
+    out = jax.ShapeDtypeStruct((members, rows, width), bf16)
+    window_raw, fast_raw = pl.pallas_call(
         functools.partial(layer_kernel, (groups, members, rows, width, pad, chunk)),
         out_shape=(out, out),
         in_specs=[anywhere] * 7 + [pl.BlockSpec(memory_space=pltpu.SMEM)],
-        out_specs=(vmem, vmem),
+        out_specs=(anywhere, anywhere),
         scratch_shapes=[
             keys, keys, pltpu.VMEM((members * rows, width), bf16),
-            pltpu.VMEM((members, 8, lanes), jnp.float32),
+            pltpu.VMEM((members, members, rows), jnp.float32),
             matrices, matrices, pltpu.VMEM((3 * width, width), jnp.float32),
-            parts, parts, parts, parts, blocks, blocks, blocks, blocks,
+            parts, parts, parts, parts, blocks, blocks,
         ]
         + [dma((members,))] * 8
         + [dma((2, members))] * 2
@@ -537,7 +603,8 @@
         cost_estimate=pl.CostEstimate(
             flops=16 * 2**30, bytes_accessed=10 * 2**20, transcendentals=4 * 2**20
         ),
-    )(key_rows, value_rows, queries, rates, fast_one, fast_three, fast_two, head_gain)
+    )(key_rows, value_rows, queries, token_rates.T, fast_one, fast_three, fast_two, head_gain)
+    return normed_rows(window_raw, fast_raw)
 
 
 def solution(mesh):
@@ -549,7 +616,8 @@
         weights = P("head", None, None)
         groups, width, rows_here = ctx // members, args[4].shape[1], args[0].shape[0] // ctx
         whole_blocks = rows_here % 64 == 0 and width % 128 == 0 and members * rows_here > WINDOW
-        fits = whole_blocks and members > 1 and groups % 2 == 0 and 3 * width // 128 >= members
+        pairs = groups % 2 == 0 and members > 1 and members & (members - 1) == 0
+        fits = whole_blocks and pairs and members % 8 == 0 and 3 * width // 128 >= members
         return jax.shard_map(
             local_kernel if fits and head == 1 else local,
             mesh=split,

time: 138 us -> 133 us (0.964)
  local copies, waits for them, and re-layouts: 5.31 us -> 0 us
    pallas_call x1, Pallas kernels: 132 us -> 127 us  [local_kernel(): pl.pallas_call(functools.partial(layer_kernel, (groups, members, rows, wi...]
    pallas_call x0 -> x1, Pallas kernels: none -> 4.75 us  [normed_rows(): pl.pallas_call(norm_kernel, grid=(rows // block,), out_shape=(out, out),...]
    unnamed x4 -> x0, local copies, waits for them, and re-layouts: 3.97 us -> none
where the time goes in v2:
time: 133 us
  Pallas kernels  132 us (99%)
    pallas_call x1, Pallas kernels, local_kernel(): pl.pallas_call(functools.partial(layer_kernel, (groups, members, rows, wi...  127 us
    pallas_call x1, Pallas kernels, normed_rows(): pl.pallas_call(norm_kernel, grid=(rows // block,), out_shape=(out, out),...  4.75 us

profile of v2, /device:TPU:1, one launch (start us, length us, event | category | flops | bytes accessed | tf_op | source)
XLA Modules:
  0.0 132.6 jit_solution(18363005568419524700)
XLA Ops:
  0.6 127.2 %shard_map.95 = (bf16[8,192,512]{2,1,0:T(8,128)(2,1)}, bf16[8,192,512]{2,1,0:T(8,128)(2,1)}) custom-call(bf16[192,4096]{1,0:T(8,128)(2,1)} %k_hbm.1, bf16[192,4096]{1,0:T(8,128)(2,1)} %v_hbm.1, bf16[192,4096]{1,0:T(8,128)(2,1)} %q_hbm.1, f32[8,192]{1,0:T(8,128)} %bitcast.1, bf16[8,512,512]{2,1,0:T(8,128)(2,1)} %one_hbm.1, bf16[8,512,512]{2,1,0:T(8,128)(2,1)} %three_hbm.1, ...), custom_call_target="tpu_custom_call" | custom-call | flops 17179869184 | bytes 10485760 | tf_op jit(solution)/shard_map/pallas_call | solution.py:584
  127.8 4.8 %shard_map.96 = (bf16[192,4096]{1,0:T(8,128)(2,1)}, bf16[192,4096]{1,0:T(8,128)(2,1)}) custom-call(bf16[8,192,512]{2,1,0:T(8,128)(2,1)} %get-tuple-element.4.window_raw, bf16[8,192,512]{2,1,0:T(8,128)(2,1)} %get-tuple-element.5.fast_raw), custom_call_target="tpu_custom_call" | custom-call | flops 6291456 | bytes 6291456 | tf_op jit(solution)/shard_map/pallas_call | solution.py:558

commit v3 on v2

--- a/solution.py
+++ b/solution.py
@@ -161,7 +161,7 @@
     dims, k_hbm, v_hbm, q_hbm, rates_hbm, one_hbm, three_hbm, two_hbm, gain_ref,
     window_recv, fast_recv,
     kbuf, vbuf, qbuf, rbuf, weights, updated, grads, from_outer, from_inner, to_inner, to_outer,
-    window_send, fast_send,
+    window_send, fast_send, units, hiddens, gates, slopes,
     k_s, k_r, v_s, v_r, q_s, q_r, r_s, r_r, halo_s, halo_r, outer_r, inner_r, inner_s, outer_s,
     win_s, win_r, fast_s, fast_r, load_sem,
 ):
@@ -321,7 +321,22 @@
 
     @pl.loop(0, members)
     def _(d):
+        here = own_rows(other_member(me, d, members))
+        there = own_rows(other_member(me, d, members), 0)
+        key_unit = rms_unit(kbuf[here])
+        a = dot_nn(key_unit, weights[0])
+        b = dot_nn(key_unit, weights[1])
+        sig = 1.0 / (1.0 + jnp.exp(-a))
+        active = a * sig
+        units[there] = key_unit
+        hiddens[there] = (active * b).astype(bf16)
+        gates[there] = active
+        slopes[there] = b * sig * (1.0 + a * (1.0 - sig))
+
+    @pl.loop(0, members)
+    def _(d):
         s = other_member(me, d, members)
+        there = own_rows(s, 0)
 
         @pl.when(d == 0)
         def _():
@@ -335,13 +350,10 @@
         def _():
             exchange(v_hbm, vbuf, base, v_s, v_r, d).wait_recv()
 
-        for_halo(1, s, jnp.logical_and(has_upper, d > 1), lambda copy: copy.start())
-
         @pl.when(d > 0)
         def _():
             exchange(q_hbm, qbuf, 0, q_s, q_r, d).start()
 
-        key_unit = rms_unit(kbuf[own_rows(s)])
         heads_rates = rbuf[s]
         is_mine = lax.broadcasted_iota(jnp.int32, heads_rates.shape, 0) == me
         rate_row = jnp.sum(jnp.where(is_mine, heads_rates, 0.0), axis=0, keepdims=True)
@@ -350,17 +362,13 @@
         )
         rate = jnp.sum(jnp.where(diagonal, rate_row, 0.0), axis=1, keepdims=True)
         delta_out = (-rate * vbuf[own_rows(s)].astype(f32)).astype(bf16)
-        a = dot_nn(key_unit, weights[0])
-        b = dot_nn(key_unit, weights[1])
         dh = dot_nt(delta_out, weights[2])
-        sig = 1.0 / (1.0 + jnp.exp(-a))
-        active = a * sig
-        hidden = (active * b).astype(bf16)
-        delta_three = (dh * active).astype(bf16)
-        delta_one = (dh * b * sig * (1.0 + a * (1.0 - sig))).astype(bf16)
+        key_unit = units[there]
+        delta_three = (dh * gates[there]).astype(bf16)
+        delta_one = (dh * slopes[there]).astype(bf16)
         grads[0:width] += dot_tn(key_unit, delta_one)
         grads[width : 2 * width] += dot_tn(key_unit, delta_three)
-        grads[2 * width : 3 * width] += dot_tn(hidden, delta_out)
+        grads[2 * width : 3 * width] += dot_tn(hiddens[there], delta_out)
 
     def rows_of(i):
         return pl.ds(pl.multiple_of(i * chunk, chunk), chunk)
@@ -420,6 +428,24 @@
             current = (COEF_A * current.astype(f32) + dot_nn(mixer, current)).astype(bf16)
         updated[m] = (weights[m].astype(f32) - current.astype(f32)).astype(bf16)
 
+    def attend_and_send(s):
+        piece = s + halo_first
+        for which in range(2):
+            for_halo(
+                which, piece, jnp.logical_and(has_lower, piece < members),
+                lambda copy: copy.wait_recv(),
+            )
+        window_send[s] = attend(s)
+
+        @pl.when(s == me)
+        def _():
+            block_kept(window_send, window_recv, win_r).start()
+
+        @pl.when(s != me)
+        def _():
+            block_to(window_send, window_recv, win_s, win_r, s).start()
+
+    halo_step = jnp.where(grp == 0, chunks - 4, jnp.where(in_lower, chunks, chunks + 1))
     per_matrix = width // chunk
     lag = 2
 
@@ -454,34 +480,26 @@
             def _():
                 orthogonal_update(j // per_matrix)
 
-        @pl.when(jnp.logical_and(i >= chunks - members, i < chunks))
-        def _():
-            s = chunks - 1 - i
-            d = other_member(me, s, members)
-
-            @pl.when(d == 0)
-            def _():
-                kept(q_hbm, qbuf, 0, q_r).wait()
-
-            @pl.when(d > 0)
-            def _():
+        @pl.when(i == halo_step)
+        def _():
+            @pl.loop(2, members)
+            def _(d):
+                for_halo(1, other_member(me, d, members), has_upper, lambda copy: copy.start())
+
+        @pl.when(i == chunks - members)
+        def _():
+            kept(q_hbm, qbuf, 0, q_r).wait()
+
+            @pl.loop(1, members)
+            def _(d):
                 exchange(q_hbm, qbuf, 0, q_s, q_r, d).wait_recv()
 
-            piece = s + halo_first
-            for which in range(2):
-                for_halo(
-                    which, piece, jnp.logical_and(has_lower, piece < members),
-                    lambda copy: copy.wait_recv(),
-                )
-            window_send[s] = attend(s)
-
-            @pl.when(s == me)
-            def _():
-                block_kept(window_send, window_recv, win_r).start()
-
-            @pl.when(s != me)
-            def _():
-                block_to(window_send, window_recv, win_s, win_r, s).start()
+        late = chunks - 1 - i
+        ready = jnp.logical_or(grp == 0, late + halo_first >= members)
+
+        @pl.when((i >= chunks - members) & (i < chunks) & ready)
+        def _():
+            attend_and_send(late)
 
     gain = gain_ref[me]
 
@@ -501,6 +519,12 @@
         @pl.when(s != me)
         def _():
             block_to(fast_send, fast_recv, fast_s, fast_r, s).start()
+
+    @pl.when(has_lower)
+    def _():
+        @pl.loop(0, members - halo_first)
+        def _(i):
+            attend_and_send(members - halo_first - 1 - i)
 
     block_kept(window_send, window_recv, win_r).wait()
     block_kept(fast_send, fast_recv, fast_r).wait()
@@ -576,6 +600,7 @@
     chunks = 3 * width // chunk
     bf16, dma = jnp.bfloat16, pltpu.SemaphoreType.DMA
     keys = pltpu.VMEM((pad + WINDOW + members * rows, width), bf16)
+    tokens = pltpu.VMEM((members * rows, width), bf16)
     parts = pltpu.VMEM((chunks, chunk, width), bf16)
     blocks = pltpu.VMEM((members, rows, width), bf16)
     matrices = pltpu.VMEM((3, width, width), bf16)
@@ -587,10 +612,12 @@
         in_specs=[anywhere] * 7 + [pl.BlockSpec(memory_space=pltpu.SMEM)],
         out_specs=(anywhere, anywhere),
         scratch_shapes=[
-            keys, keys, pltpu.VMEM((members * rows, width), bf16),
+            keys, keys, tokens,
             pltpu.VMEM((members, members, rows), jnp.float32),
             matrices, matrices, pltpu.VMEM((3 * width, width), jnp.float32),
             parts, parts, parts, parts, blocks, blocks,
+            tokens, tokens, pltpu.VMEM((members * rows, width), jnp.float32),
+            pltpu.VMEM((members * rows, width), jnp.float32),
         ]
         + [dma((members,))] * 8
         + [dma((2, members))] * 2

time: 133 us -> 135 us (1.015)
  the two profiles are of different devices: /device:TPU:1 before, /device:TPU:24 now
where the time goes in v3:
time: 135 us
  Pallas kernels  134 us (99%)
    pallas_call x1, Pallas kernels, local_kernel(): pl.pallas_call(functools.partial(layer_kernel, (groups, members, rows, wi...  129 us
    pallas_call x1, Pallas kernels, normed_rows(): pl.pallas_call(norm_kernel, grid=(rows // block,), out_shape=(out, out),...  4.75 us

profile of v3, /device:TPU:24, one launch (start us, length us, event | category | flops | bytes accessed | tf_op | source)
XLA Modules:
  0.0 134.7 jit_solution(15535002591536962185)
XLA Ops:
  0.6 129.3 %shard_map.95 = (bf16[8,192,512]{2,1,0:T(8,128)(2,1)}, bf16[8,192,512]{2,1,0:T(8,128)(2,1)}) custom-call(bf16[192,4096]{1,0:T(8,128)(2,1)} %k_hbm.1, bf16[192,4096]{1,0:T(8,128)(2,1)} %v_hbm.1, bf16[192,4096]{1,0:T(8,128)(2,1)} %q_hbm.1, f32[8,192]{1,0:T(8,128)} %bitcast.1, bf16[8,512,512]{2,1,0:T(8,128)(2,1)} %one_hbm.1, bf16[8,512,512]{2,1,0:T(8,128)(2,1)} %three_hbm.1, ...), custom_call_target="tpu_custom_call" | custom-call | flops 17179869184 | bytes 10485760 | tf_op jit(solution)/shard_map/pallas_call | solution.py:609
  130.0 4.8 %shard_map.96 = (bf16[192,4096]{1,0:T(8,128)(2,1)}, bf16[192,4096]{1,0:T(8,128)(2,1)}) custom-call(bf16[8,192,512]{2,1,0:T(8,128)(2,1)} %get-tuple-element.4.window_raw, bf16[8,192,512]{2,1,0:T(8,128)(2,1)} %get-tuple-element.5.fast_raw), custom_call_target="tpu_custom_call" | custom-call | flops 6291456 | bytes 6291456 | tf_op jit(solution)/shard_map/pallas_call | solution.py:582
